TPU v7x, 256 devices: a whole 4x4x8 slice. The times are simulated.
256 devices in a mesh: dp: 32 (over y, z), mp: 8 (over x, core).
Axes of the slice: x: 4, y: 4, z: 8, core: 2. Of those that a mesh axis runs over, the one named last changes fastest.
Arguments:
- tokens: bfloat16 [4096, 4096], P('dp', 'mp'), may hold values from -6 to 6
- cotangent: bfloat16 [4096, 4096], P('dp', 'mp'), may hold values from -6 to 6
- language: int32 [4096, 1], P('dp'), may hold values from 0 to 7; in each aligned block of 128 rows (0 to 127, 128 to 255, ...) at most 24 rows name the same one
- owner: int32 [8], replicated, may hold values from 0 to 7, each once
- w_in: bfloat16 [4096, 65536], P(None, ('dp', 'mp')), may hold values from -0.09375 to 0.09375
- w_out: bfloat16 [65536, 4096], P(('dp', 'mp')), may hold values from -0.0625 to 0.0625
Outputs:
- ffn_out: bfloat16 [4096, 4096], P('dp', 'mp')
- grad_tokens: bfloat16 [4096, 4096], P('dp', 'mp')
- grad_in: bfloat16 [4096, 65536], P(None, ('dp', 'mp'))
- grad_out: bfloat16 [65536, 4096], P(('dp', 'mp'))
Inputs may be any that keep to these rules, and one draw needn't show every extreme that they name: In each aligned block of 128 rows (the rows of one index of dp) no language appears more than 24 times; some language appears exactly 24 times in some block; every language appears somewhere. `owner`: each slot 0 to 7 belongs to exactly one language.
All inputs are finite; a program needn't handle non-finite values.
Results may differ from a plain program's by a relative error of at most 0.019.
Values may be sent and summed in bfloat16 or wider, within the bound.
A program may use at most 128 MiB of HBM per device.

v0:
```python
import jax
import jax.numpy as jnp
from jax import lax
from jax.sharding import PartitionSpec as P

ROOT_HALF = 0.7071067811865476
INV_ROOT_TAU = 0.3989422804014327


def gelu_pair(hidden):
    normal_cdf = 0.5 * (1.0 + lax.erf(hidden * ROOT_HALF))
    return (
        hidden * normal_cdf,
        normal_cdf + hidden * jnp.exp(-0.5 * hidden * hidden) * INV_ROOT_TAU,
    )


def shards(tokens, cotangent, language, owner, w_in, w_out):
    peer_count = lax.axis_size("dp")
    lang_count = owner.shape[0]
    group_size = peer_count // lang_count
    row_count = tokens.shape[0]
    capacity = 3 * row_count // (2 * lang_count)
    slot_rows = peer_count * capacity
    row_lang = language[:, 0]
    lang_ids = jnp.arange(lang_count, dtype=jnp.int32)
    lang_hit = (row_lang[:, None] == lang_ids[None, :]).astype(jnp.int32)
    slot_row = jnp.sum(lang_hit * owner[None, :], axis=1)
    slot_hit = (slot_row[:, None] == lang_ids[None, :]).astype(jnp.int32)
    row_rank = jnp.sum((jnp.cumsum(slot_hit, axis=0) - 1) * slot_hit, axis=1)
    row_cell = slot_row * capacity + row_rank
    placing = jnp.arange(lang_count * capacity, dtype=jnp.int32)[:, None] == row_cell[None, :]
    place_half = placing.astype(jnp.bfloat16)
    place_full = placing.astype(jnp.float32)

    def pack_rows(values):
        packed = jnp.dot(place_half, values, preferred_element_type=jnp.float32).astype(
            jnp.bfloat16
        )
        packed = packed.reshape(lang_count, 1, capacity, values.shape[1])
        packed = jnp.broadcast_to(packed, (lang_count, group_size, capacity, values.shape[1]))
        return packed.reshape(peer_count, capacity, values.shape[1])

    def fold_group(values):
        summed = jnp.sum(
            values.astype(jnp.float32).reshape(lang_count, group_size, capacity, values.shape[2]),
            axis=1,
        )
        return summed.reshape(lang_count * capacity, values.shape[2])

    def unpack_rows(values):
        return lax.dot_general(
            place_full,
            values,
            (((0,), (0,)), ((), ())),
            precision=lax.Precision.HIGHEST,
            preferred_element_type=jnp.float32,
        )

    whole_x, whole_g = (
        lax.all_gather(tokens, "mp", axis=1, tiled=True),
        lax.all_gather(cotangent, "mp", axis=1, tiled=True),
    )
    sent_x, sent_g = (
        lax.all_to_all(pack_rows(whole_x), "dp", split_axis=0, concat_axis=0, tiled=True),
        lax.all_to_all(pack_rows(whole_g), "dp", split_axis=0, concat_axis=0, tiled=True),
    )
    inputs = sent_x.reshape(slot_rows, sent_x.shape[2])
    cotans = sent_g.reshape(slot_rows, sent_g.shape[2])
    hidden = jnp.dot(inputs, w_in, preferred_element_type=jnp.float32)
    act_value, act_slope = gelu_pair(hidden)
    act = act_value.astype(jnp.bfloat16)
    act_grad = lax.dot_general(
        cotans, w_out, (((1,), (1,)), ((), ())), preferred_element_type=jnp.float32
    )
    hidden_grad = (act_grad * act_slope).astype(jnp.bfloat16)
    grad_in = lax.dot_general(
        inputs, hidden_grad, (((0,), (0,)), ((), ())), preferred_element_type=jnp.float32
    ).astype(jnp.bfloat16)
    grad_out = lax.dot_general(
        act, cotans, (((0,), (0,)), ((), ())), preferred_element_type=jnp.float32
    ).astype(jnp.bfloat16)
    out_term = jnp.dot(act, w_out, preferred_element_type=jnp.float32)
    back_term = lax.dot_general(
        hidden_grad, w_in, (((1,), (1,)), ((), ())), preferred_element_type=jnp.float32
    )
    out_half = out_term.astype(jnp.bfloat16).reshape(peer_count, capacity, out_term.shape[1])
    back_half = back_term.astype(jnp.bfloat16).reshape(peer_count, capacity, back_term.shape[1])
    out_home, back_home = (
        lax.all_to_all(out_half, "dp", split_axis=0, concat_axis=0, tiled=True),
        lax.all_to_all(back_half, "dp", split_axis=0, concat_axis=0, tiled=True),
    )
    full_out = unpack_rows(fold_group(out_home))
    full_back = unpack_rows(fold_group(back_home))
    ffn_out, grad_tokens = (
        lax.psum_scatter(
            full_out.astype(jnp.bfloat16), "mp", scatter_dimension=1, tiled=True
        ).astype(jnp.float32),
        lax.psum_scatter(
            full_back.astype(jnp.bfloat16), "mp", scatter_dimension=1, tiled=True
        ).astype(jnp.float32),
    )
    return (ffn_out.astype(jnp.bfloat16), grad_tokens.astype(jnp.bfloat16), grad_in, grad_out)


def solution(mesh):
    placed = (
        P("dp", "mp"),
        P("dp", "mp"),
        P("dp", None),
        P(),
        P(None, ("dp", "mp")),
        P(("dp", "mp"), None),
    )
    return jax.shard_map(
        shards,
        mesh=mesh,
        in_specs=placed,
        out_specs=(P("dp", "mp"), P("dp", "mp"), P(None, ("dp", "mp")), P(("dp", "mp"), None)),
        check_vma=False,
    )
```

profile of v0, /device:TPU:42, one launch (start us, length us, event | category | flops | bytes accessed | tf_op | source)
XLA Modules:
  0.0 693.8 jit_solution(495798699579012026)
XLA Ops:
  7.2 0.0 copy-start
  7.2 0.0 all-gather.3.cloned.1.call-start
  7.2 0.7 all-gather.3.cloned.1.call-update
  7.9 0.8 select_reduce_fusion.1
  8.8 0.1 fusion.5
  8.9 0.2 reduce_window_sum.11
  9.0 0.2 select_reduce_fusion
  9.2 27.4 %all-gather.3.cloned.1.call-done = bf16[128,4096]{1,0:T(8,128)(2,1)} async-done(((bf16[128,512]{1,0:T(8,128)(2,1)}), bf16[128,4096]{1,0:T(8,128)(2,1)}) %all-gather.3.cloned.1.call-update) | async-done | bytes 1048592 | tf_op jit(solution)/shard_map/all_gather | solution.py:61
  36.6 1.8 convolution_convert_fusion.5
  38.4 3.4 broadcast_in_dim.9
  41.8 10.1 %all-to-all-start = ((bf16[32,24,4096]{2,1,0:T(8,128)(2,1)}), bf16[32,24,4096]{2,1,0:T(8,128)(2,1)}, u32[]{:S(2)}, u32[]{:S(2)}) async-start(bf16[32,24,4096]{2,1,0:T(8,128)(2,1)} %bitcast.33), calls=%async_computation | async-start | bytes 12582912 | tf_op jit(solution)/shard_map/all_to_all | solution.py:65
  52.0 0.0 all-gather.5.cloned.1.call-start
  52.0 0.7 all-gather.5.cloned.1.call-update
  52.7 27.4 %all-gather.5.cloned.1.call-done = bf16[128,4096]{1,0:T(8,128)(2,1)} async-done(((bf16[128,512]{1,0:T(8,128)(2,1)}), bf16[128,4096]{1,0:T(8,128)(2,1)}) %all-gather.5.cloned.1.call-update) | async-done | bytes 1048592 | tf_op jit(solution)/shard_map/all_gather | solution.py:62
  80.2 2.9 convolution_convert_fusion.4
  83.1 107.2 %all-to-all-done = bf16[32,24,4096]{2,1,0:T(8,128)(2,1)} async-done(((bf16[32,24,4096]{2,1,0:T(8,128)(2,1)}), bf16[32,24,4096]{2,1,0:T(8,128)(2,1)}, u32[]{:S(2)}, u32[]{:S(2)}) %all-to-all-start) | async-done | bytes 6291488 | tf_op jit(solution)/shard_map/all_to_all | solution.py:65
  190.3 4.8 broadcast_in_dim.11
  195.1 12.2 %all-to-all-start.2 = ((bf16[32,24,4096]{2,1,0:T(8,128)(2,1)}), bf16[32,24,4096]{2,1,0:T(8,128)(2,1)}, u32[]{:S(2)}, u32[]{:S(2)}) async-start(bf16[32,24,4096]{2,1,0:T(8,128)(2,1)} %bitcast.34), calls=%async_computation.3 | async-start | bytes 12582912 | tf_op jit(solution)/shard_map/all_to_all | solution.py:66
  207.3 5.2 fusion.10
  212.5 0.0 copy-done
  212.5 4.5 convolution_convert_fusion.1
  217.0 128.9 %all-to-all-done.2 = bf16[32,24,4096]{2,1,0:T(8,128)(2,1)} async-done(((bf16[32,24,4096]{2,1,0:T(8,128)(2,1)}), bf16[32,24,4096]{2,1,0:T(8,128)(2,1)}, u32[]{:S(2)}, u32[]{:S(2)}) %all-to-all-start.2) | async-done | bytes 6291488 | tf_op jit(solution)/shard_map/all_to_all | solution.py:66
  345.9 11.1 %all-to-all-start.1 = ((bf16[32,24,4096]{2,1,0:T(8,128)(2,1)}), bf16[32,24,4096]{2,1,0:T(8,128)(2,1)}, u32[]{:S(2)}, u32[]{:S(2)}) async-start(bf16[32,24,4096]{2,1,0:T(8,128)(2,1)} %bitcast.32), calls=%async_computation.1 | async-start | bytes 12582912 | tf_op jit(solution)/shard_map/all_to_all | solution.py:90
  357.0 0.0 copy-start.2
  357.0 4.9 fusion
  361.9 0.0 copy-done.2
  361.9 4.4 convolution_convert_fusion
  366.3 129.3 %all-to-all-done.1 = bf16[32,24,4096]{2,1,0:T(8,128)(2,1)} async-done(((bf16[32,24,4096]{2,1,0:T(8,128)(2,1)}), bf16[32,24,4096]{2,1,0:T(8,128)(2,1)}, u32[]{:S(2)}, u32[]{:S(2)}) %all-to-all-start.1) | async-done | bytes 6291488 | tf_op jit(solution)/shard_map/all_to_all | solution.py:90
  495.6 12.5 %all-to-all-start.3 = ((bf16[32,24,4096]{2,1,0:T(8,128)(2,1)}), bf16[32,24,4096]{2,1,0:T(8,128)(2,1)}, u32[]{:S(2)}, u32[]{:S(2)}) async-start(bf16[32,24,4096]{2,1,0:T(8,128)(2,1)} %bitcast.31), calls=%async_computation.4 | async-start | bytes 12582912 | tf_op jit(solution)/shard_map/all_to_all | solution.py:91
  508.1 0.2 reduce-scatter.3.cloned.1.call-start
  508.4 4.3 convert_reduce_fusion.1
  512.7 2.5 convolution_convert_fusion.7
  515.2 0.0 reduce-scatter.3.cloned.1.call-update
  515.2 0.0 reduce-scatter.5.cloned.1.call-start
  515.2 131.3 %all-to-all-done.3 = bf16[32,24,4096]{2,1,0:T(8,128)(2,1)} async-done(((bf16[32,24,4096]{2,1,0:T(8,128)(2,1)}), bf16[32,24,4096]{2,1,0:T(8,128)(2,1)}, u32[]{:S(2)}, u32[]{:S(2)}) %all-to-all-start.3) | async-done | bytes 6291488 | tf_op jit(solution)/shard_map/all_to_all | solution.py:91
  646.5 4.3 convert_reduce_fusion
  650.8 2.5 convolution_convert_fusion.6
  653.4 0.0 reduce-scatter.5.cloned.1.call-update
  653.4 6.0 convolution_convert_fusion.2
  659.4 0.0 copy-start.1
  659.4 6.1 convolution_convert_fusion.3
  665.5 0.0 reduce-scatter.3.cloned.1.call-done
  665.5 21.8 %reduce-scatter.5.cloned.1.call-done = bf16[128,512]{1,0:T(8,128)(2,1)} async-done(((bf16[128,4096]{1,0:T(8,128)(2,1)}), bf16[128,512]{1,0:T(8,128)(2,1)}) %reduce-scatter.5.cloned.1.call-update) | async-done | bytes 131088 | tf_op jit(solution)/shard_map/reduce_scatter | solution.py:99
  687.3 0.0 copy-done.1
  (1 shorter events, 0.0 us)
Async XLA Ops:
  7.2 205.3 %copy-start = (bf16[256,4096]{1,0:T(8,128)(2,1)S(1)}, bf16[256,4096]{1,0:T(8,128)(2,1)}, u32[]{:S(2)}) copy-start(bf16[256,4096]{1,0:T(8,128)(2,1)} %param.11) | copy-start | bytes 6291460
  7.2 29.4 %all-gather.3.cloned.1.call-start = ((), (), s32[]{:S(2)}) async-start(), calls=%async_computation.6 | async-start | bytes 1179648 | tf_op jit(solution)/shard_map/all_gather | solution.py:61
  41.8 148.5 %all-to-all-start = ((bf16[32,24,4096]{2,1,0:T(8,128)(2,1)}), bf16[32,24,4096]{2,1,0:T(8,128)(2,1)}, u32[]{:S(2)}, u32[]{:S(2)}) async-start(bf16[32,24,4096]{2,1,0:T(8,128)(2,1)} %bitcast.33), calls=%async_computation | async-start | bytes 12582912 | tf_op jit(solution)/shard_map/all_to_all | solution.py:65
  52.0 28.2 %all-gather.5.cloned.1.call-start = ((), (), s32[]{:S(2)}) async-start(), calls=%async_computation.8 | async-start | bytes 1179648 | tf_op jit(solution)/shard_map/all_gather | solution.py:62
  195.1 150.8 %all-to-all-start.2 = ((bf16[32,24,4096]{2,1,0:T(8,128)(2,1)}), bf16[32,24,4096]{2,1,0:T(8,128)(2,1)}, u32[]{:S(2)}, u32[]{:S(2)}) async-start(bf16[32,24,4096]{2,1,0:T(8,128)(2,1)} %bitcast.34), calls=%async_computation.3 | async-start | bytes 12582912 | tf_op jit(solution)/shard_map/all_to_all | solution.py:66
  345.9 149.7 %all-to-all-start.1 = ((bf16[32,24,4096]{2,1,0:T(8,128)(2,1)}), bf16[32,24,4096]{2,1,0:T(8,128)(2,1)}, u32[]{:S(2)}, u32[]{:S(2)}) async-start(bf16[32,24,4096]{2,1,0:T(8,128)(2,1)} %bitcast.32), calls=%async_computation.1 | async-start | bytes 12582912 | tf_op jit(solution)/shard_map/all_to_all | solution.py:90
  357.0 4.9 copy-start.2
  495.6 150.9 %all-to-all-start.3 = ((bf16[32,24,4096]{2,1,0:T(8,128)(2,1)}), bf16[32,24,4096]{2,1,0:T(8,128)(2,1)}, u32[]{:S(2)}, u32[]{:S(2)}) async-start(bf16[32,24,4096]{2,1,0:T(8,128)(2,1)} %bitcast.31), calls=%async_computation.4 | async-start | bytes 12582912 | tf_op jit(solution)/shard_map/all_to_all | solution.py:91
  508.1 157.3 %reduce-scatter.3.cloned.1.call-start = ((), (), s32[]{:S(2)}) async-start(), calls=%async_computation.7 | async-start | bytes 1179648 | tf_op jit(solution)/shard_map/reduce_scatter | solution.py:96
  515.2 172.1 %reduce-scatter.5.cloned.1.call-start = ((), (), s32[]{:S(2)}) async-start(), calls=%async_computation.9 | async-start | bytes 1179648 | tf_op jit(solution)/shard_map/reduce_scatter | solution.py:99
  659.4 27.9 %copy-start.1 = (bf16[256,4096]{1,0:T(8,128)(2,1)S(1)}, bf16[256,4096]{1,0:T(8,128)(2,1)}, u32[]{:S(2)}) copy-start(bf16[256,4096]{1,0:T(8,128)(2,1)} %param.11) | copy-start | bytes 6291460
Sparse Core Ops, SparseCore 0:
  9.9 26.7 all-gather.2
  54.6 25.4 all-gather.4
  515.3 32.1 reduce-scatter.2
  653.5 33.7 reduce-scatter.4
where the time goes:
time: 698 us; the launch traced here: 694 us
  waiting for transfers between devices  575 us (82%)
  starting transfers between devices  46.2 us (7%)
  matrix products  40.9 us (6%)
  between operations  13.9 us (2%)
  other arithmetic  9.84 us (1%)
  local copies, waits for them, and re-layouts  8.24 us (1%)
    all_to_all x1, waiting for transfers between devices, shards(): lax.all_to_all(back_half, 'dp', split_axis=0, concat_axis=0, tiled=True)  131 us
    all_to_all x1, waiting for transfers between devices, shards(): lax.all_to_all(out_half, 'dp', split_axis=0, concat_axis=0, tiled=True)  129 us
    all_to_all x1, waiting for transfers between devices, shards(): lax.all_to_all(pack_rows(whole_g), 'dp', split_axis=0, concat_axis=0, til...  129 us
    all_to_all x1, waiting for transfers between devices, shards(): lax.all_to_all(pack_rows(whole_x), 'dp', split_axis=0, concat_axis=0, til...  107 us
    all_gather x1, waiting for transfers between devices, shards(): lax.all_gather(cotangent, 'mp', axis=1, tiled=True)  27.4 us
    all_gather x1, waiting for transfers between devices, shards(): lax.all_gather(tokens, 'mp', axis=1, tiled=True)  27.4 us
    reduce_scatter x1, waiting for transfers between devices, shards(): lax.psum_scatter(full_back.astype(jnp.bfloat16), 'mp', scatter_dimension=...  21.8 us
  transfers between devices with their start and end apart: 8, of which 7 were waited for; matrix products, arithmetic and copies ran while one was open for 7% of the time, Pallas kernels for 0%

commit v1 on v0

v1 whole, which is shorter than its diff:
```python
import jax
import jax.numpy as jnp
from jax import lax
from jax.experimental import pallas as pl
from jax.experimental.pallas import tpu as pltpu
from jax.sharding import PartitionSpec as P

MESH = pl.DeviceIdType.MESH
ROOT_HALF = 0.7071067811865476
INV_ROOT_TAU = 0.3989422804014327

NY, NZ, NX, NC = 4, 8, 4, 2
NP = NX * NC
BF = jnp.bfloat16
F32 = jnp.float32


def gelu_pair(hidden):
    normal_cdf = 0.5 * (1.0 + lax.erf(hidden * ROOT_HALF))
    return (
        hidden * normal_cdf,
        normal_cdf + hidden * jnp.exp(-0.5 * hidden * hidden) * INV_ROOT_TAU,
    )


def z_step(i):
    return ((i + 1) // 2) * (2 * (i % 2) - 1)


def nt_dot(a, b):
    return lax.dot_general(a, b, (((1,), (1,)), ((), ())), preferred_element_type=F32)


def kernel(
    tok, cot, lang, owner, w_in, w_out,
    ffn, gtok, grad_in, grad_out,
    w1, w2, pack, yrecv, zsend, gath, act, hgrad, part, srecv, acc, xrecv, zrecv, ysend, yback,
    gi, go,
    w_sem, g_sem, y_sem, z_sem, x_sem, s_sem, ps_sem, px_sem, pz_sem, py_sem,
):
    dp, mp = lax.axis_index("dp"), lax.axis_index("mp")
    y, z = dp // NZ, dp % NZ
    x, c = mp // NC, mp % NC
    rows, feat = tok.shape
    cell_rows = pack.shape[1]
    cap = cell_rows // 2
    chunk = NY * cap
    half = chunk // 2
    xr, xl, xo = (x + 1) % NX, (x + NX - 1) % NX, (x + 2) % NX
    sib = {"dp": dp, "mp": x * NC + 1 - c}
    right = {"dp": dp, "mp": xr * NC + c}
    left = {"dp": dp, "mp": xl * NC + c}

    def at_y(k):
        return {"dp": ((y + k) % NY) * NZ + z, "mp": mp}

    def at_z(k):
        return {"dp": y * NZ + (z + k + NZ) % NZ, "mp": mp}

    def remote(src, dst, sems, where, device):
        return pltpu.make_async_remote_copy(
            src_ref=src,
            dst_ref=dst,
            send_sem=sems.at[(0, *where)],
            recv_sem=sems.at[(1, *where)],
            device_id=device,
            device_id_type=MESH,
        )

    load1 = pltpu.make_async_copy(w_in, w1, w_sem.at[0])
    load2 = pltpu.make_async_copy(w_out, w2, w_sem.at[1])
    load1.start()
    load2.start()

    barrier = pltpu.get_barrier_semaphore()
    partners = [sib, right, left]
    partners += [at_y(k) for k in range(1, NY)] + [at_z(k) for k in range(1, NZ)]
    for device in partners:
        pl.semaphore_signal(barrier, inc=1, device_id=device, device_id_type=MESH)

    langs = owner.shape[1]
    hit = lang[...] == lax.broadcasted_iota(jnp.int32, (rows, langs), 1)
    lower = (
        lax.broadcasted_iota(jnp.int32, (rows, rows), 1)
        < lax.broadcasted_iota(jnp.int32, (rows, rows), 0)
    )
    before = jnp.dot(
        jnp.where(lower, 1.0, 0.0).astype(BF),
        jnp.where(hit, 1.0, 0.0).astype(BF),
        preferred_element_type=F32,
    )
    cell = jnp.sum(
        jnp.where(hit, before + owner[...].astype(F32) * cap, 0.0), axis=1, keepdims=True
    )
    cells = langs * cap
    place = jnp.where(
        cell.astype(jnp.int32) == lax.broadcasted_iota(jnp.int32, (rows, cells), 1), 1.0, 0.0
    )
    place_t = jnp.transpose(place).astype(BF)
    place = place.astype(BF)
    packed_x = jnp.dot(place_t, tok[...], preferred_element_type=F32).astype(BF)
    packed_g = jnp.dot(place_t, cot[...], preferred_element_type=F32).astype(BF)
    pack[:, :, :feat] = packed_x.reshape(NY, cell_rows, feat)
    pack[:, :, feat:] = packed_g.reshape(NY, cell_rows, feat)

    pl.semaphore_wait(barrier, len(partners))

    def y_copy(k):
        return remote(pack.at[(y + k) % NY], yrecv.at[k], y_sem, (k,), at_y(k))

    for k in range(1, NY):
        y_copy(k).start()
    yrecv[0] = pack[y]
    for k in range(1, NY):
        y_copy(k).wait_recv()
    for h in range(2):
        for col in (0, feat):
            block = jnp.concatenate(
                [
                    yrecv[k, :, col : col + feat].astype(F32)[h * cap : (h + 1) * cap]
                    for k in range(NY)
                ],
                axis=0,
            ).astype(BF)
            zsend[h, :, :, col : col + feat] = block.reshape(2, half, feat)

    half_z = NZ // 2

    def z_copy(i):
        to = (z - z_step(i) + NZ) % NZ
        return remote(
            zsend.at[to // half_z], gath.at[i, mp], z_sem, (i,), {"dp": y * NZ + to, "mp": mp}
        )

    @pl.loop(1, NZ)
    def _(i):
        z_copy(i).start()

    gath[0, mp] = zsend[z // half_z]

    def g_copy(kind, i):
        if kind == 0:
            return remote(gath.at[i, mp], gath.at[i, mp], x_sem, (0, i), right)
        if kind == 1:
            return remote(gath.at[i, mp], gath.at[i, mp], x_sem, (1, i), left)
        if kind == 2:
            src = gath.at[i, xl * NC + c, 0]
            return remote(src, src, x_sem, (2, i), right)
        src = gath.at[i, xr * NC + c, 1]
        return remote(src, src, x_sem, (3, i), left)

    def s_copy(kind, i):
        src = gath.at[i, (x, xl, xr, xo)[kind] * NC + c]
        return remote(src, src, s_sem, (kind, i), sib)

    def ps_copy(i):
        return remote(part.at[i], srecv.at[i], ps_sem, (i,), sib)

    def p_copy(kind, i):
        where, h, device = (
            (xo, 0, right), (xo, 1, left), (xr, 1, right), (xl, 0, left), (xr, 0, right), (xl, 1, left),
        )[kind]
        return remote(acc.at[i, where, h], xrecv.at[i, kind], px_sem, (kind, i), device)

    def pz_copy(i):
        return remote(acc.at[i, x], zrecv.at[z], pz_sem, (i,), at_z(z_step(i)))

    def pieces(i, p, col):
        return gath[i, p, :, :, col : col + feat].reshape(chunk, feat)

    def w_cols(p):
        return w2[:, pl.ds(pl.multiple_of(p * feat, feat), feat)]

    def w_rows(p):
        return w1[pl.ds(pl.multiple_of(p * feat, feat), feat), :]

    def compute(i):
        width = w1.shape[1]
        hidden = jnp.zeros((chunk, width), F32)
        for p in range(NP):
            hidden += jnp.dot(
                pieces(i, p, 0), w1[p * feat : (p + 1) * feat, :], preferred_element_type=F32
            )
        value, slope = gelu_pair(hidden)
        act[i] = value.astype(BF)
        back = jnp.zeros((chunk, width), F32)
        for p in range(NP):
            back += nt_dot(pieces(i, p, feat), w2[:, p * feat : (p + 1) * feat])
        hgrad[i] = (back * slope).astype(BF)
        for q in range(NX):
            p = q * NC + 1 - c
            out = jnp.dot(act[i], w_cols(p), preferred_element_type=F32)
            part[i, q, :, :, :feat] = out.astype(BF).reshape(2, half, feat)
            out = nt_dot(hgrad[i], w_rows(p))
            part[i, q, :, :, feat:] = out.astype(BF).reshape(2, half, feat)

    def own_part(i):
        for q in range(NX):
            p = q * NC + c
            out = jnp.dot(act[i], w_cols(p), preferred_element_type=F32).reshape(2, half, feat)
            out += srecv[i, q, :, :, :feat].astype(F32)
            acc[i, q, :, :, :feat] = out.astype(BF)
            out = nt_dot(hgrad[i], w_rows(p)).reshape(2, half, feat)
            out += srecv[i, q, :, :, feat:].astype(F32)
            acc[i, q, :, :, feat:] = out.astype(BF)

    def add_to(i, where, h, kinds):
        for col in (0, feat):
            total = acc[i, where, h, :, col : col + feat].astype(F32)
            for kind in kinds:
                total += xrecv[i, kind, :, col : col + feat].astype(F32)
            acc[i, where, h, :, col : col + feat] = total.astype(BF)

    def grads(p):
        hg_t = jnp.transpose(hgrad[...].reshape(NZ * chunk, -1).astype(F32)).astype(BF)
        act_t = jnp.transpose(act[...].reshape(NZ * chunk, -1).astype(F32)).astype(BF)
        xs = gath[:, p, :, :, :feat].reshape(NZ * chunk, feat)
        gs = gath[:, p, :, :, feat:].reshape(NZ * chunk, feat)
        first = jnp.dot(hg_t, xs, preferred_element_type=F32)
        gi[p] = jnp.transpose(first).astype(BF)
        go[p] = jnp.dot(act_t, gs, preferred_element_type=F32).astype(BF)

    def gi_copy(p):
        start = pl.multiple_of(p * feat, feat)
        return pltpu.make_async_copy(gi.at[p], grad_in.at[pl.ds(start, feat), :], g_sem.at[0, p])

    def go_copy(p):
        start = pl.multiple_of(p * feat, feat)
        return pltpu.make_async_copy(go.at[p], grad_out.at[:, pl.ds(start, feat)], g_sem.at[1, p])

    load1.wait()
    load2.wait()

    def stage(t, after):
        return (t >= after) & (t < NZ + after)

    @pl.loop(0, NZ + 6)
    def _(t):
        @pl.when((t >= 1) & (t < NZ))
        def _():
            z_copy(t).wait_recv()

        @pl.when(stage(t, 0))
        def _():
            g_copy(0, t).start()
            g_copy(1, t).start()
            s_copy(0, t).start()

        @pl.when(stage(t, 1))
        def _():
            i = t - 1
            g_copy(0, i).wait_recv()
            g_copy(2, i).start()
            s_copy(1, i).start()
            g_copy(1, i).wait_recv()
            g_copy(3, i).start()
            s_copy(2, i).start()

        @pl.when(stage(t, 2))
        def _():
            i = t - 2
            g_copy(2, i).wait_recv()
            g_copy(3, i).wait_recv()
            s_copy(3, i).start()

        @pl.when(stage(t, 5))
        def _():
            i = t - 5
            p_copy(0, i).wait_recv()
            add_to(i, xr, 0, (0,))
            p_copy(4, i).start()
            p_copy(1, i).wait_recv()
            add_to(i, xl, 1, (1,))
            p_copy(5, i).start()

        @pl.when(stage(t, 4))
        def _():
            i = t - 4
            ps_copy(i).wait_recv()
            own_part(i)
            for kind in range(4):
                p_copy(kind, i).start()

        @pl.when(stage(t, 3))
        def _():
            i = t - 3
            for kind in range(4):
                s_copy(kind, i).wait_recv()
            compute(i)
            ps_copy(i).start()

        @pl.when(stage(t, 6))
        def _():
            i = t - 6
            for kind in range(2, 6):
                p_copy(kind, i).wait_recv()
            add_to(i, x, 0, (3, 4))
            add_to(i, x, 1, (2, 5))

            @pl.when(i > 0)
            def _():
                pz_copy(i).start()

            @pl.when(i == 0)
            def _():
                zrecv[z] = acc[0, x]

        @pl.when(t >= NZ + 3)
        def _():
            for k in range(3):
                p = (t - NZ - 3) * 3 + k

                @pl.when(p < NP)
                def _():
                    grads(p)
                    gi_copy(p).start()
                    go_copy(p).start()

    @pl.loop(1, NZ)
    def _(i):
        pz_copy(i).wait_recv()

    for col in (0, feat):
        sums = []
        for h in range(2):
            total = zrecv[h * half_z, :, :, col : col + feat].astype(F32)
            for k in range(1, half_z):
                total += zrecv[h * half_z + k, :, :, col : col + feat].astype(F32)
            sums.append(total.reshape(chunk, feat))
        for k in range(NY):
            block = jnp.concatenate([s[k * cap : (k + 1) * cap] for s in sums], axis=0)
            ysend[k, :, col : col + feat] = block.astype(BF)

    def yb_copy(k):
        return remote(ysend.at[k], yback.at[y], py_sem, (k,), at_y(NY - k))

    for k in range(1, NY):
        yb_copy(k).start()
    yback[y] = ysend[0]
    for k in range(1, NY):
        yb_copy(k).wait_recv()
    home = yback[...].reshape(cells, 2 * feat)
    ffn[...] = jnp.dot(place, home[:, :feat], preferred_element_type=F32).astype(BF)
    gtok[...] = jnp.dot(place, home[:, feat:], preferred_element_type=F32).astype(BF)

    for k in range(1, NY):
        y_copy(k).wait_send()
        yb_copy(k).wait_send()

    @pl.loop(1, NZ)
    def _(i):
        z_copy(i).wait_send()
        pz_copy(i).wait_send()

    @pl.loop(0, NZ)
    def _(i):
        for kind in range(4):
            g_copy(kind, i).wait_send()
            s_copy(kind, i).wait_send()
        ps_copy(i).wait_send()
        for kind in range(6):
            p_copy(kind, i).wait_send()

    @pl.loop(0, NP)
    def _(p):
        gi_copy(p).wait()
        go_copy(p).wait()


def shards(tokens, cotangent, language, owner, w_in, w_out):
    rows, feat = tokens.shape
    depth, width = w_in.shape
    langs = owner.shape[0]
    cap = 3 * rows // (2 * langs)
    chunk = NY * cap
    half = chunk // 2
    vmem, hbm = pl.BlockSpec(memory_space=pltpu.VMEM), pl.BlockSpec(memory_space=pl.ANY)
    dma = pltpu.SemaphoreType.DMA
    return pl.pallas_call(
        kernel,
        out_shape=(
            jax.ShapeDtypeStruct((rows, feat), BF),
            jax.ShapeDtypeStruct((rows, feat), BF),
            jax.ShapeDtypeStruct((depth, width), BF),
            jax.ShapeDtypeStruct((width, depth), BF),
        ),
        in_specs=[vmem] * 4 + [hbm] * 2,
        out_specs=(vmem, vmem, hbm, hbm),
        scratch_shapes=[
            pltpu.VMEM((depth, width), BF),
            pltpu.VMEM((width, depth), BF),
            pltpu.VMEM((NY, 2 * cap, 2 * feat), BF),
            pltpu.VMEM((NY, 2 * cap, 2 * feat), BF),
            pltpu.VMEM((2, 2, half, 2 * feat), BF),
            pltpu.VMEM((NZ, NP, 2, half, 2 * feat), BF),
            pltpu.VMEM((NZ, chunk, width), BF),
            pltpu.VMEM((NZ, chunk, width), BF),
            pltpu.VMEM((NZ, NX, 2, half, 2 * feat), BF),
            pltpu.VMEM((NZ, NX, 2, half, 2 * feat), BF),
            pltpu.VMEM((NZ, NX, 2, half, 2 * feat), BF),
            pltpu.VMEM((NZ, 6, half, 2 * feat), BF),
            pltpu.VMEM((NZ, 2, half, 2 * feat), BF),
            pltpu.VMEM((NY, 2 * cap, 2 * feat), BF),
            pltpu.VMEM((NY, 2 * cap, 2 * feat), BF),
            pltpu.VMEM((NP, feat, width), BF),
            pltpu.VMEM((NP, width, feat), BF),
            dma((2,)),
            dma((2, NP)),
            dma((2, NY)),
            dma((2, NZ)),
            dma((2, 4, NZ)),
            dma((2, 4, NZ)),
            dma((2, NZ)),
            dma((2, 6, NZ)),
            dma((2, NZ)),
            dma((2, NY)),
        ],
        compiler_params=pltpu.CompilerParams(
            collective_id=0, has_side_effects=True, vmem_limit_bytes=60 * 1024 * 1024
        ),
        cost_estimate=pl.CostEstimate(
            flops=12 * NZ * chunk * depth * width, bytes_accessed=16 * depth * width, transcendentals=0
        ),
    )(tokens, cotangent, language, owner.reshape(1, langs), w_in, w_out)


def solution(mesh):
    placed = (
        P("dp", "mp"),
        P("dp", "mp"),
        P("dp", None),
        P(),
        P(None, ("dp", "mp")),
        P(("dp", "mp"), None),
    )
    return jax.shard_map(
        shards,
        mesh=mesh,
        in_specs=placed,
        out_specs=(P("dp", "mp"), P("dp", "mp"), P(None, ("dp", "mp")), P(("dp", "mp"), None)),
        check_vma=False,
    )
```

time: 698 us -> 161 us (0.23)
  the two profiles are of different devices: /device:TPU:42 before, /device:TPU:104 now
where the time goes in v1:
time: 161 us
  Pallas kernels  151 us (94%)
  local copies, waits for them, and re-layouts  9.04 us (6%)
    pallas_call x1, Pallas kernels, shards(): pl.pallas_call(kernel, out_shape=(jax.ShapeDtypeStruct((rows, feat), BF),...  151 us
    unnamed x7, local copies, waits for them, and re-layouts  9.04 us

profile of v1, /device:TPU:104, one launch (start us, length us, event | category | flops | bytes accessed | tf_op | source)
XLA Modules:
  0.0 160.8 jit_solution(2084606544729222431)
XLA Ops:
  0.6 1.4 copy.10.lang
  2.0 151.1 %shard_map.93 = (bf16[128,512]{1,0:T(8,128)(2,1)}, bf16[128,512]{1,0:T(8,128)(2,1)}, bf16[4096,256]{1,0:T(8,128)(2,1)}, bf16[256,4096]{1,0:T(8,128)(2,1)}) custom-call(bf16[128,512]{1,0:T(8,128)(2,1)} %tok.1, bf16[128,512]{1,0:T(8,128)(2,1)} %cot.1, s32[128,1]{1,0:T(8,128)} %copy.10.lang, s32[1,8]{1,0:T(1,128)} %bitcast.1, bf16[4096,256]{1,0:T(8,128)(2,1)} %w_in.1, ...), custom_call_target="tpu_custom_call" | custom-call | flops 9663676416 | bytes 16777216 | tf_op jit(solution)/shard_map/pallas_call | solution.py:379
  153.1 1.6 copy.15
  154.7 1.6 copy.16
  156.3 0.0 copy-start
  156.3 3.2 %copy.17 = bf16[4096,256]{1,0:T(8,128)(2,1)} copy(bf16[4096,256]{1,0:T(8,128)(2,1)} %get-tuple-element.10) | data formatting | bytes 4194304
  159.5 0.0 copy-done
  159.5 1.3 copy.18
Async XLA Ops:
  156.3 3.2 %copy-start = (bf16[256,4096]{1,0:T(8,128)(2,1)S(1)}, bf16[256,4096]{1,0:T(8,128)(2,1)}, u32[]{:S(2)}) copy-start(bf16[256,4096]{1,0:T(8,128)(2,1)} %get-tuple-element.11) | copy-start | bytes 6291460

commit v2 on v1

--- a/solution.py
+++ b/solution.py
@@ -23,8 +23,9 @@
     )
 
 
-def z_step(i):
-    return ((i + 1) // 2) * (2 * (i % 2) - 1)
+def back_order(e):
+    order = (4, 3, 7, 6, 5, 2, 1, 0)
+    return sum(i * ((e - k + 8) // 8) * ((k - e + 8) // 8) for k, i in enumerate(order))
 
 
 def nt_dot(a, b):
@@ -34,9 +35,10 @@
 def kernel(
     tok, cot, lang, owner, w_in, w_out,
     ffn, gtok, grad_in, grad_out,
-    w1, w2, pack, yrecv, zsend, gath, act, hgrad, part, srecv, acc, xrecv, zrecv, ysend, yback,
-    gi, go,
-    w_sem, g_sem, y_sem, z_sem, x_sem, s_sem, ps_sem, px_sem, pz_sem, py_sem,
+    w1, w2, pack, yrecv, zsend, gath, act, hgrad, part, srecv, acc, xrecv, frecv, qrecv, zrecv,
+    ysend, yback, gi, go,
+    w_sem, g_sem, y_sem, z_sem, f_sem, q_sem, x_sem, s_sem, ps_sem, px_sem, fr_sem, qr_sem, pz_sem,
+    py_sem,
 ):
     dp, mp = lax.axis_index("dp"), lax.axis_index("mp")
     y, z = dp // NZ, dp % NZ
@@ -50,6 +52,7 @@
     sib = {"dp": dp, "mp": x * NC + 1 - c}
     right = {"dp": dp, "mp": xr * NC + c}
     left = {"dp": dp, "mp": xl * NC + c}
+    ez = 1 - 2 * (z % 2)
 
     def at_y(k):
         return {"dp": ((y + k) % NY) * NZ + z, "mp": mp}
@@ -73,31 +76,33 @@
     load2.start()
 
     barrier = pltpu.get_barrier_semaphore()
-    partners = [sib, right, left]
-    partners += [at_y(k) for k in range(1, NY)] + [at_z(k) for k in range(1, NZ)]
+    partners = [sib, right, left] + [at_y(k) for k in range(1, NY)]
+    partners += [at_z(k * ez) for k in (1, -1, 2, -2, -3)]
     for device in partners:
         pl.semaphore_signal(barrier, inc=1, device_id=device, device_id_type=MESH)
 
     langs = owner.shape[1]
-    hit = lang[...] == lax.broadcasted_iota(jnp.int32, (rows, langs), 1)
-    lower = (
-        lax.broadcasted_iota(jnp.int32, (rows, rows), 1)
-        < lax.broadcasted_iota(jnp.int32, (rows, rows), 0)
+    hit = lang[...] == lax.broadcasted_iota(jnp.int32, (langs, rows), 0)
+    upper = (
+        lax.broadcasted_iota(jnp.int32, (rows, rows), 0)
+        < lax.broadcasted_iota(jnp.int32, (rows, rows), 1)
     )
     before = jnp.dot(
-        jnp.where(lower, 1.0, 0.0).astype(BF),
         jnp.where(hit, 1.0, 0.0).astype(BF),
+        jnp.where(upper, 1.0, 0.0).astype(BF),
         preferred_element_type=F32,
     )
-    cell = jnp.sum(
-        jnp.where(hit, before + owner[...].astype(F32) * cap, 0.0), axis=1, keepdims=True
-    )
+    diagonal = lax.broadcasted_iota(jnp.int32, (langs, langs), 0) == lax.broadcasted_iota(
+        jnp.int32, (langs, langs), 1
+    )
+    slots = jnp.sum(jnp.where(diagonal, owner[...].astype(F32), 0.0), axis=1, keepdims=True)
+    cell = jnp.sum(jnp.where(hit, before + slots * cap, 0.0), axis=0, keepdims=True)
     cells = langs * cap
-    place = jnp.where(
-        cell.astype(jnp.int32) == lax.broadcasted_iota(jnp.int32, (rows, cells), 1), 1.0, 0.0
-    )
-    place_t = jnp.transpose(place).astype(BF)
-    place = place.astype(BF)
+    place_t = jnp.where(
+        cell.astype(jnp.int32) == lax.broadcasted_iota(jnp.int32, (cells, rows), 0), 1.0, 0.0
+    )
+    place = jnp.transpose(place_t).astype(BF)
+    place_t = place_t.astype(BF)
     packed_x = jnp.dot(place_t, tok[...], preferred_element_type=F32).astype(BF)
     packed_g = jnp.dot(place_t, cot[...], preferred_element_type=F32).astype(BF)
     pack[:, :, :feat] = packed_x.reshape(NY, cell_rows, feat)
@@ -125,17 +130,24 @@
             zsend[h, :, :, col : col + feat] = block.reshape(2, half, feat)
 
     half_z = NZ // 2
-
-    def z_copy(i):
-        to = (z - z_step(i) + NZ) % NZ
-        return remote(
-            zsend.at[to // half_z], gath.at[i, mp], z_sem, (i,), {"dp": y * NZ + to, "mp": mp}
-        )
-
-    @pl.loop(1, NZ)
-    def _(i):
-        z_copy(i).start()
-
+    pair = at_z(ez)
+
+    def z_copy(k):
+        to = (z + (0, -ez, 2 * ez, -3 * ez)[k] + NZ) % NZ
+        device = {"dp": y * NZ + to, "mp": mp}
+        return remote(zsend.at[to // half_z], gath.at[2 * k - 1, mp], z_sem, (k,), device)
+
+    def z_arrived(k):
+        return remote(zsend.at[0], gath.at[2 * k - 1, mp], z_sem, (k,), pair)
+
+    def f_copy(k):
+        return remote(gath.at[2 * k - 1, mp], gath.at[2 * k, mp], f_sem, (k,), pair)
+
+    def q_copy(kind):
+        p = (x, xl, xr, xo)[kind] * NC + c
+        return remote(gath.at[0, p], gath.at[NZ - 1, p], q_sem, (kind,), pair)
+
+    z_copy(1).start()
     gath[0, mp] = zsend[z // half_z]
 
     def g_copy(kind, i):
@@ -162,8 +174,14 @@
         )[kind]
         return remote(acc.at[i, where, h], xrecv.at[i, kind], px_sem, (kind, i), device)
 
-    def pz_copy(i):
-        return remote(acc.at[i, x], zrecv.at[z], pz_sem, (i,), at_z(z_step(i)))
+    def fr_copy(k):
+        return remote(acc.at[2 * k, x], frecv.at[k], fr_sem, (k,), pair)
+
+    def qr_copy(q):
+        return remote(acc.at[NZ - 1, q], qrecv.at[q], qr_sem, (q,), pair)
+
+    def pz_copy(k):
+        return remote(acc.at[2 * k - 1, x], zrecv.at[z // 2], pz_sem, (k,), at_z(-k * ez))
 
     def pieces(i, p, col):
         return gath[i, p, :, :, col : col + feat].reshape(chunk, feat)
@@ -187,6 +205,8 @@
         for p in range(NP):
             back += nt_dot(pieces(i, p, feat), w2[:, p * feat : (p + 1) * feat])
         hgrad[i] = (back * slope).astype(BF)
+
+    def sib_part(i):
         for q in range(NX):
             p = q * NC + 1 - c
             out = jnp.dot(act[i], w_cols(p), preferred_element_type=F32)
@@ -204,6 +224,13 @@
             out += srecv[i, q, :, :, feat:].astype(F32)
             acc[i, q, :, :, feat:] = out.astype(BF)
 
+    def add_pair(i, q, ref):
+        for h in range(2):
+            for col in (0, feat):
+                total = acc[i, q, h, :, col : col + feat].astype(F32)
+                total += ref[h, :, col : col + feat].astype(F32)
+                acc[i, q, h, :, col : col + feat] = total.astype(BF)
+
     def add_to(i, where, h, kinds):
         for col in (0, feat):
             total = acc[i, where, h, :, col : col + feat].astype(F32)
@@ -231,22 +258,37 @@
     load1.wait()
     load2.wait()
 
-    def stage(t, after):
-        return (t >= after) & (t < NZ + after)
-
-    @pl.loop(0, NZ + 6)
+    def stage(t, after, count=NZ):
+        return (t >= after) & (t < count + after)
+
+    last = NZ - 1
+    first_back = NZ - 1
+
+    @pl.loop(0, NZ + first_back + 3)
     def _(t):
-        @pl.when((t >= 1) & (t < NZ))
-        def _():
-            z_copy(t).wait_recv()
-
-        @pl.when(stage(t, 0))
+        @pl.when((t >= 2) & (t < last) & (t % 2 == 0))
+        def _():
+            f_copy(t // 2).wait_recv()
+
+        @pl.when(stage(t, 0, last))
         def _():
             g_copy(0, t).start()
             g_copy(1, t).start()
             s_copy(0, t).start()
 
-        @pl.when(stage(t, 1))
+        @pl.when((t < last - 1) & (t % 2 == 0))
+        def _():
+            k = t // 2 + 1
+            z_arrived(k).wait_recv()
+            f_copy(k).start()
+
+        for k in (1, 2):
+
+            @pl.when(t == 2 * k - 2)
+            def _():
+                z_copy(k + 1).start()
+
+        @pl.when(stage(t, 1, last))
         def _():
             i = t - 1
             g_copy(0, i).wait_recv()
@@ -256,76 +298,125 @@
             g_copy(3, i).start()
             s_copy(2, i).start()
 
-        @pl.when(stage(t, 2))
+        @pl.when(stage(t, 2, last))
         def _():
             i = t - 2
             g_copy(2, i).wait_recv()
             g_copy(3, i).wait_recv()
             s_copy(3, i).start()
 
-        @pl.when(stage(t, 5))
-        def _():
-            i = t - 5
-            p_copy(0, i).wait_recv()
-            add_to(i, xr, 0, (0,))
-            p_copy(4, i).start()
-            p_copy(1, i).wait_recv()
-            add_to(i, xl, 1, (1,))
-            p_copy(5, i).start()
-
-        @pl.when(stage(t, 4))
-        def _():
-            i = t - 4
+        for kind in range(4):
+
+            @pl.when(t == 3 + kind)
+            def _():
+                q_copy(kind).start()
+
+        @pl.when(t == last + 1)
+        def _():
+            for kind in range(4):
+                q_copy(kind).wait_recv()
+                s_copy(kind, last).start()
+
+        @pl.when(stage(t, first_back + 4))
+        def _():
+            i = back_order(t - first_back - 4)
+
+            @pl.when((i < last) & (i % 2 == 1))
+            def _():
+                k = (i + 1) // 2
+                fr_copy(k).wait_recv()
+                add_pair(i, x, frecv.at[k])
+                pz_copy(k).start()
+
+        @pl.when(stage(t, first_back + 1))
+        def _():
+            i = back_order(t - first_back - 1)
             ps_copy(i).wait_recv()
             own_part(i)
-            for kind in range(4):
-                p_copy(kind, i).start()
-
-        @pl.when(stage(t, 3))
+
+            @pl.when(i == 0)
+            def _():
+                for q in range(NX):
+                    qr_copy(q).wait_recv()
+                    add_pair(0, q, qrecv.at[q])
+
+            @pl.when(i < last)
+            def _():
+                for kind in range(4):
+                    p_copy(kind, i).start()
+
+        @pl.when(stage(t, first_back + 2))
+        def _():
+            i = back_order(t - first_back - 2)
+
+            @pl.when(i < last)
+            def _():
+                p_copy(0, i).wait_recv()
+                add_to(i, xr, 0, (0,))
+                p_copy(4, i).start()
+                p_copy(1, i).wait_recv()
+                add_to(i, xl, 1, (1,))
+                p_copy(5, i).start()
+
+        for q in range(NX):
+
+            @pl.when(t == last + 3 + q)
+            def _():
+                qr_copy(q).start()
+
+        @pl.when(stage(t, 3, last))
         def _():
             i = t - 3
             for kind in range(4):
                 s_copy(kind, i).wait_recv()
             compute(i)
+
+        @pl.when(t == last + 2)
+        def _():
+            for kind in range(4):
+                s_copy(kind, last).wait_recv()
+            compute(last)
+
+        @pl.when(stage(t, first_back))
+        def _():
+            i = back_order(t - first_back)
+            sib_part(i)
             ps_copy(i).start()
 
-        @pl.when(stage(t, 6))
-        def _():
-            i = t - 6
-            for kind in range(2, 6):
-                p_copy(kind, i).wait_recv()
-            add_to(i, x, 0, (3, 4))
-            add_to(i, x, 1, (2, 5))
-
-            @pl.when(i > 0)
-            def _():
-                pz_copy(i).start()
+        @pl.when(stage(t, first_back + 3))
+        def _():
+            i = back_order(t - first_back - 3)
+
+            @pl.when(i < last)
+            def _():
+                for kind in range(2, 6):
+                    p_copy(kind, i).wait_recv()
+                add_to(i, x, 0, (3, 4))
+                add_to(i, x, 1, (2, 5))
+
+            @pl.when((i > 0) & (i % 2 == 0))
+            def _():
+                fr_copy(i // 2).start()
 
             @pl.when(i == 0)
             def _():
-                zrecv[z] = acc[0, x]
-
-        @pl.when(t >= NZ + 3)
-        def _():
-            for k in range(3):
-                p = (t - NZ - 3) * 3 + k
-
-                @pl.when(p < NP)
-                def _():
-                    grads(p)
-                    gi_copy(p).start()
-                    go_copy(p).start()
-
-    @pl.loop(1, NZ)
-    def _(i):
-        pz_copy(i).wait_recv()
+                zrecv[z // 2] = acc[0, x]
+
+        @pl.when(stage(t, NZ + 2))
+        def _():
+            p = t - NZ - 2
+            grads(p)
+            gi_copy(p).start()
+            go_copy(p).start()
+
+    for k in (1, 2, 3):
+        pz_copy(k).wait_recv()
 
     for col in (0, feat):
         sums = []
         for h in range(2):
-            total = zrecv[h * half_z, :, :, col : col + feat].astype(F32)
-            for k in range(1, half_z):
-                total += zrecv[h * half_z + k, :, :, col : col + feat].astype(F32)
+            total = zrecv[2 * h, :, :, col : col + feat].astype(F32)
+            total += zrecv[2 * h + 1, :, :, col : col + feat].astype(F32)
             sums.append(total.reshape(chunk, feat))
         for k in range(NY):
             block = jnp.concatenate([s[k * cap : (k + 1) * cap] for s in sums], axis=0)
@@ -347,17 +438,25 @@
         y_copy(k).wait_send()
         yb_copy(k).wait_send()
 
-    @pl.loop(1, NZ)
-    def _(i):
-        z_copy(i).wait_send()
-        pz_copy(i).wait_send()
+        z_copy(k).wait_send()
+        f_copy(k).wait_send()
+        fr_copy(k).wait_send()
+        pz_copy(k).wait_send()
+    for kind in range(4):
+        q_copy(kind).wait_send()
+    for q in range(NX):
+        qr_copy(q).wait_send()
 
     @pl.loop(0, NZ)
     def _(i):
         for kind in range(4):
-            g_copy(kind, i).wait_send()
             s_copy(kind, i).wait_send()
         ps_copy(i).wait_send()
+
+    @pl.loop(0, last)
+    def _(i):
+        for kind in range(4):
+            g_copy(kind, i).wait_send()
         for kind in range(6):
             p_copy(kind, i).wait_send()
 
@@ -365,6 +464,28 @@
     def _(p):
         gi_copy(p).wait()
         go_copy(p).wait()
+
+
+def hand_over(a0, a1, a2, a3, b0, b1, b2, b3, v0, v1, v2, v3, sems):
+    moves = []
+    for k, (src, mid, dst) in enumerate(((a2, v2, b2), (a3, v3, b3), (a0, v0, b0), (a1, v1, b1))):
+        parts = 4 if k < 2 else 1
+        size = src.shape[0] // parts
+        for n in range(parts):
+            rows = pl.ds(n * size, size)
+            moves.append(
+                (
+                    pltpu.make_async_copy(src.at[rows], mid.at[rows], sems.at[0, k, n]),
+                    pltpu.make_async_copy(mid.at[rows], dst.at[rows], sems.at[1, k, n]),
+                )
+            )
+    for first, _ in moves:
+        first.start()
+    for first, second in moves:
+        first.wait()
+        second.start()
+    for _, second in moves:
+        second.wait()
 
 
 def shards(tokens, cotangent, language, owner, w_in, w_out):
@@ -376,7 +497,7 @@
     half = chunk // 2
     vmem, hbm = pl.BlockSpec(memory_space=pltpu.VMEM), pl.BlockSpec(memory_space=pl.ANY)
     dma = pltpu.SemaphoreType.DMA
-    return pl.pallas_call(
+    results = pl.pallas_call(
         kernel,
         out_shape=(
             jax.ShapeDtypeStruct((rows, feat), BF),
@@ -399,7 +520,9 @@
             pltpu.VMEM((NZ, NX, 2, half, 2 * feat), BF),
             pltpu.VMEM((NZ, NX, 2, half, 2 * feat), BF),
             pltpu.VMEM((NZ, 6, half, 2 * feat), BF),
-            pltpu.VMEM((NZ, 2, half, 2 * feat), BF),
+            pltpu.VMEM((4, 2, half, 2 * feat), BF),
+            pltpu.VMEM((NX, 2, half, 2 * feat), BF),
+            pltpu.VMEM((NZ // 2, 2, half, 2 * feat), BF),
             pltpu.VMEM((NY, 2 * cap, 2 * feat), BF),
             pltpu.VMEM((NY, 2 * cap, 2 * feat), BF),
             pltpu.VMEM((NP, feat, width), BF),
@@ -407,12 +530,16 @@
             dma((2,)),
             dma((2, NP)),
             dma((2, NY)),
-            dma((2, NZ)),
+            dma((2, 4)),
+            dma((2, 4)),
+            dma((2, 4)),
             dma((2, 4, NZ)),
             dma((2, 4, NZ)),
             dma((2, NZ)),
             dma((2, 6, NZ)),
-            dma((2, NZ)),
+            dma((2, 4)),
+            dma((2, NX)),
+            dma((2, 4)),
             dma((2, NY)),
         ],
         compiler_params=pltpu.CompilerParams(
@@ -421,7 +548,15 @@
         cost_estimate=pl.CostEstimate(
             flops=12 * NZ * chunk * depth * width, bytes_accessed=16 * depth * width, transcendentals=0
         ),
-    )(tokens, cotangent, language, owner.reshape(1, langs), w_in, w_out)
+    )(tokens, cotangent, language.reshape(1, rows), owner.reshape(1, langs), w_in, w_out)
+    return pl.pallas_call(
+        hand_over,
+        out_shape=tuple(jax.ShapeDtypeStruct(r.shape, r.dtype) for r in results),
+        in_specs=[hbm] * 4,
+        out_specs=(hbm,) * 4,
+        scratch_shapes=[pltpu.VMEM(r.shape, r.dtype) for r in results] + [dma((2, 4, 4))],
+        compiler_params=pltpu.CompilerParams(vmem_limit_bytes=60 * 1024 * 1024),
+    )(*results)
 
 
 def solution(mesh):

time: 161 us -> 144 us (0.89)
  the two profiles are of different devices: /device:TPU:104 before, /device:TPU:42 now
where the time goes in v2:
time: 144 us
  Pallas kernels  143 us (99%)
    pallas_call x1, Pallas kernels, shards(): pl.pallas_call(kernel, out_shape=(jax.ShapeDtypeStruct((rows, feat), BF),...  139 us
    pallas_call x1, Pallas kernels, shards(): pl.pallas_call(hand_over, out_shape=tuple((jax.ShapeDtypeStruct(r.shape,...  3.85 us

profile of v2, /device:TPU:42, one launch (start us, length us, event | category | flops | bytes accessed | tf_op | source)
XLA Modules:
  0.0 143.9 jit_solution(13287303130007468121)
XLA Ops:
  0.6 139.4 %shard_map.93 = (bf16[128,512]{1,0:T(8,128)(2,1)}, bf16[128,512]{1,0:T(8,128)(2,1)}, bf16[4096,256]{1,0:T(8,128)(2,1)}, bf16[256,4096]{1,0:T(8,128)(2,1)}) custom-call(bf16[128,512]{1,0:T(8,128)(2,1)} %tok.1, bf16[128,512]{1,0:T(8,128)(2,1)} %cot.1, s32[1,128]{1,0:T(1,128)} %bitcast.2, s32[1,8]{1,0:T(1,128)} %bitcast.3, bf16[4096,256]{1,0:T(8,128)(2,1)} %w_in.1, ...), custom_call_target="tpu_custom_call" | custom-call | flops 9663676416 | bytes 16777216 | tf_op jit(solution)/shard_map/pallas_call | solution.py:500
  140.0 3.9 %shard_map.94 = (bf16[128,512]{1,0:T(8,128)(2,1)}, bf16[128,512]{1,0:T(8,128)(2,1)}, bf16[4096,256]{1,0:T(8,128)(2,1)}, bf16[256,4096]{1,0:T(8,128)(2,1)}) custom-call(bf16[128,512]{1,0:T(8,128)(2,1)} %get-tuple-element.8.a0, bf16[128,512]{1,0:T(8,128)(2,1)} %get-tuple-element.9.a1, bf16[4096,256]{1,0:T(8,128)(2,1)} %get-tuple-element.10.a2, ...), custom_call_target="tpu_custom_call" | custom-call | tf_op jit(solution)/shard_map/pallas_call | solution.py:552

commit v3 on v2

--- a/solution.py
+++ b/solution.py
@@ -24,7 +24,7 @@
 
 
 def back_order(e):
-    order = (4, 3, 7, 6, 5, 2, 1, 0)
+    order = (4, 7, 3, 6, 5, 2, 1, 0)
     return sum(i * ((e - k + 8) // 8) * ((k - e + 8) // 8) for k, i in enumerate(order))
 
 
@@ -266,27 +266,44 @@
 
     @pl.loop(0, NZ + first_back + 3)
     def _(t):
+        @pl.when(stage(t, first_back + 1))
+        def _():
+            i = back_order(t - first_back - 1)
+            ps_copy(i).wait_recv()
+            own_part(i)
+
+            @pl.when(i == 0)
+            def _():
+                for q in range(NX):
+                    qr_copy(q).wait_recv()
+                    add_pair(0, q, qrecv.at[q])
+
+            @pl.when(i < last)
+            def _():
+                for kind in range(4):
+                    p_copy(kind, i).start()
+
         @pl.when((t >= 2) & (t < last) & (t % 2 == 0))
         def _():
             f_copy(t // 2).wait_recv()
+
+        @pl.when((t < last) & (t % 2 == 1))
+        def _():
+            k = (t + 1) // 2
+            z_arrived(k).wait_recv()
+            f_copy(k).start()
+
+        for k in (2, 3):
+
+            @pl.when(t == k)
+            def _():
+                z_copy(k).start()
 
         @pl.when(stage(t, 0, last))
         def _():
             g_copy(0, t).start()
             g_copy(1, t).start()
             s_copy(0, t).start()
-
-        @pl.when((t < last - 1) & (t % 2 == 0))
-        def _():
-            k = t // 2 + 1
-            z_arrived(k).wait_recv()
-            f_copy(k).start()
-
-        for k in (1, 2):
-
-            @pl.when(t == 2 * k - 2)
-            def _():
-                z_copy(k + 1).start()
 
         @pl.when(stage(t, 1, last))
         def _():
@@ -307,11 +324,11 @@
 
         for kind in range(4):
 
-            @pl.when(t == 3 + kind)
+            @pl.when(t == min(3 + kind, 5))
             def _():
                 q_copy(kind).start()
 
-        @pl.when(t == last + 1)
+        @pl.when(t == last)
         def _():
             for kind in range(4):
                 q_copy(kind).wait_recv()
@@ -327,23 +344,6 @@
                 fr_copy(k).wait_recv()
                 add_pair(i, x, frecv.at[k])
                 pz_copy(k).start()
-
-        @pl.when(stage(t, first_back + 1))
-        def _():
-            i = back_order(t - first_back - 1)
-            ps_copy(i).wait_recv()
-            own_part(i)
-
-            @pl.when(i == 0)
-            def _():
-                for q in range(NX):
-                    qr_copy(q).wait_recv()
-                    add_pair(0, q, qrecv.at[q])
-
-            @pl.when(i < last)
-            def _():
-                for kind in range(4):
-                    p_copy(kind, i).start()
 
         @pl.when(stage(t, first_back + 2))
         def _():
@@ -360,7 +360,7 @@
 
         for q in range(NX):
 
-            @pl.when(t == last + 3 + q)
+            @pl.when(t == last + 2 + q)
             def _():
                 qr_copy(q).start()
 
@@ -371,7 +371,7 @@
                 s_copy(kind, i).wait_recv()
             compute(i)
 
-        @pl.when(t == last + 2)
+        @pl.when(t == last + 1)
         def _():
             for kind in range(4):
                 s_copy(kind, last).wait_recv()

time: 144 us -> 138 us (0.958)
  Pallas kernels: 143 us -> 136 us
    pallas_call x1, Pallas kernels: 139 us -> 132 us  [shards(): pl.pallas_call(kernel, out_shape=(jax.ShapeDtypeStruct((rows, feat), BF),...]
where the time goes in v3:
time: 138 us; the launch traced here: 137 us
  Pallas kernels  136 us (99%)
    pallas_call x1, Pallas kernels, shards(): pl.pallas_call(kernel, out_shape=(jax.ShapeDtypeStruct((rows, feat), BF),...  132 us
    pallas_call x1, Pallas kernels, shards(): pl.pallas_call(hand_over, out_shape=tuple((jax.ShapeDtypeStruct(r.shape,...  3.85 us

profile of v3, /device:TPU:42, one launch (start us, length us, event | category | flops | bytes accessed | tf_op | source)
XLA Modules:
  0.0 136.7 jit_solution(3756902628580612086)
XLA Ops:
  0.6 132.2 %shard_map.93 = (bf16[128,512]{1,0:T(8,128)(2,1)}, bf16[128,512]{1,0:T(8,128)(2,1)}, bf16[4096,256]{1,0:T(8,128)(2,1)}, bf16[256,4096]{1,0:T(8,128)(2,1)}) custom-call(bf16[128,512]{1,0:T(8,128)(2,1)} %tok.1, bf16[128,512]{1,0:T(8,128)(2,1)} %cot.1, s32[1,128]{1,0:T(1,128)} %bitcast.2, s32[1,8]{1,0:T(1,128)} %bitcast.3, bf16[4096,256]{1,0:T(8,128)(2,1)} %w_in.1, ...), custom_call_target="tpu_custom_call" | custom-call | flops 9663676416 | bytes 16777216 | tf_op jit(solution)/shard_map/pallas_call | solution.py:500
  132.9 3.9 %shard_map.94 = (bf16[128,512]{1,0:T(8,128)(2,1)}, bf16[128,512]{1,0:T(8,128)(2,1)}, bf16[4096,256]{1,0:T(8,128)(2,1)}, bf16[256,4096]{1,0:T(8,128)(2,1)}) custom-call(bf16[128,512]{1,0:T(8,128)(2,1)} %get-tuple-element.8.a0, bf16[128,512]{1,0:T(8,128)(2,1)} %get-tuple-element.9.a1, bf16[4096,256]{1,0:T(8,128)(2,1)} %get-tuple-element.10.a2, ...), custom_call_target="tpu_custom_call" | custom-call | tf_op jit(solution)/shard_map/pallas_call | solution.py:552

commit v4 on v3

--- a/solution.py
+++ b/solution.py
@@ -24,7 +24,7 @@
 
 
 def back_order(e):
-    order = (4, 7, 3, 6, 5, 2, 1, 0)
+    order = (4, 7, 2, 6, 3, 5, 1, 0)
     return sum(i * ((e - k + 8) // 8) * ((k - e + 8) // 8) for k, i in enumerate(order))
 
 

time: 138 us -> 141 us (1.022)
  Pallas kernels: 136 us -> 139 us
    pallas_call x1, Pallas kernels: 132 us -> 135 us  [shards(): pl.pallas_call(kernel, out_shape=(jax.ShapeDtypeStruct((rows, feat), BF),...]
where the time goes in v4:
time: 141 us; the launch traced here: 139 us
  Pallas kernels  139 us (99%)
    pallas_call x1, Pallas kernels, shards(): pl.pallas_call(kernel, out_shape=(jax.ShapeDtypeStruct((rows, feat), BF),...  135 us
    pallas_call x1, Pallas kernels, shards(): pl.pallas_call(hand_over, out_shape=tuple((jax.ShapeDtypeStruct(r.shape,...  3.85 us

profile of v4, /device:TPU:42, one launch (start us, length us, event | category | flops | bytes accessed | tf_op | source)
XLA Modules:
  0.0 139.2 jit_solution(7395448228448129571)
XLA Ops:
  0.6 134.7 %shard_map.93 = (bf16[128,512]{1,0:T(8,128)(2,1)}, bf16[128,512]{1,0:T(8,128)(2,1)}, bf16[4096,256]{1,0:T(8,128)(2,1)}, bf16[256,4096]{1,0:T(8,128)(2,1)}) custom-call(bf16[128,512]{1,0:T(8,128)(2,1)} %tok.1, bf16[128,512]{1,0:T(8,128)(2,1)} %cot.1, s32[1,128]{1,0:T(1,128)} %bitcast.2, s32[1,8]{1,0:T(1,128)} %bitcast.3, bf16[4096,256]{1,0:T(8,128)(2,1)} %w_in.1, ...), custom_call_target="tpu_custom_call" | custom-call | flops 9663676416 | bytes 16777216 | tf_op jit(solution)/shard_map/pallas_call | solution.py:500
  135.3 3.9 %shard_map.94 = (bf16[128,512]{1,0:T(8,128)(2,1)}, bf16[128,512]{1,0:T(8,128)(2,1)}, bf16[4096,256]{1,0:T(8,128)(2,1)}, bf16[256,4096]{1,0:T(8,128)(2,1)}) custom-call(bf16[128,512]{1,0:T(8,128)(2,1)} %get-tuple-element.8.a0, bf16[128,512]{1,0:T(8,128)(2,1)} %get-tuple-element.9.a1, bf16[4096,256]{1,0:T(8,128)(2,1)} %get-tuple-element.10.a2, ...), custom_call_target="tpu_custom_call" | custom-call | tf_op jit(solution)/shard_map/pallas_call | solution.py:552
